TPU v7x, 32 devices: a whole 2x2x4 slice. The times are simulated.
32 devices in a mesh: tm: 4 (over y, x), dp: 8 (over z, core).
Axes of the slice: x: 2, y: 2, z: 4, core: 2. Of those that a mesh axis runs over, the one named last changes fastest.
Arguments:
- clips: bfloat16 [8, 16, 32, 64, 128], P('dp', 'tm'), may hold values from -6 to 6
- weight: bfloat16 [3, 3, 3, 128, 256], replicated, may hold values from -0.109375 to 0.109375
- bias: float32 [256], replicated, may hold values from -3 to 3
- out_grad: bfloat16 [8, 8, 16, 32, 256], P('dp', 'tm'), may hold values from -6 to 6
Outputs:
- features: bfloat16 [8, 8, 16, 32, 256], P('dp', 'tm')
- clips_grad: bfloat16 [8, 16, 32, 64, 128], P('dp', 'tm')
- weight_grad: float32 [3, 3, 3, 128, 256], replicated
- bias_grad: float32 [256], replicated
All inputs are finite; a program needn't handle non-finite values.
Results may differ from a plain program's by a relative error of at most 0.005.
Values may be sent and summed in bfloat16 or wider, within the bound.
A program may use at most 64 MiB of HBM per device.

v0:
```python
import math

import jax
import jax.numpy as jnp
from jax import lax
from jax.sharding import PartitionSpec as P


def passed_along(value, axis, steps):
    count = lax.axis_size(axis)
    first, last = (max(0, -steps), min(count, count - steps))
    return lax.ppermute(value, axis, [(source, source + steps) for source in range(first, last)])


def forward_conv(extended, weight):
    return lax.conv_general_dilated(
        extended,
        weight,
        (2, 2, 2),
        ((0, 0), (1, 1), (1, 1)),
        dimension_numbers=("NDHWC", "DHWIO", "NDHWC"),
        preferred_element_type=jnp.float32,
    )


def back_conv(grads, weight, low, high):
    flipped = weight[::-1, ::-1, ::-1]
    return lax.conv_general_dilated(
        grads,
        flipped,
        (1, 1, 1),
        ((low, high), (1, 2), (1, 2)),
        lhs_dilation=(2, 2, 2),
        dimension_numbers=("NDHWC", "DHWOI", "NDHWC"),
        preferred_element_type=jnp.float32,
    )


def kernel_conv(extended, pre_grad):
    return lax.conv_general_dilated(
        extended,
        pre_grad,
        (1, 1, 1),
        ((0, -1), (1, 0), (1, 0)),
        rhs_dilation=(2, 2, 2),
        dimension_numbers=("CDHWN", "IDHWO", "DHWNC"),
        preferred_element_type=jnp.float32,
    )


def local(clips, weight, bias, out_grad):
    frames = clips.shape[1]
    tail = clips[:, frames - 2 :]
    prior = passed_along(tail, "tm", 1)
    extended = jnp.concatenate([prior, clips], axis=1)
    pre = forward_conv(extended, weight) + bias
    sig = jax.nn.sigmoid(pre)
    features = (pre * sig).astype(jnp.bfloat16)
    pre_grad = (out_grad.astype(jnp.float32) * (sig * (1.0 + pre * (1.0 - sig)))).astype(
        jnp.bfloat16
    )
    own_grad = back_conv(pre_grad, weight, 0, 3)
    first_frame = passed_along(pre_grad[:, :1], "tm", -1)
    spill = back_conv(first_frame, weight, 2, 1)
    spill_full = jnp.pad(spill, ((0, 0), (frames - 2, 0), (0, 0), (0, 0), (0, 0)))
    clips_grad = (own_grad + spill_full).astype(jnp.bfloat16)
    kernel_part = kernel_conv(extended, pre_grad)
    bias_part = jnp.sum(pre_grad.astype(jnp.float32), axis=(0, 1, 2, 3))
    kernel_sum, bias_sum = lax.psum((kernel_part, bias_part), ("tm", "dp"))
    total = (
        pre_grad.shape[0]
        * pre_grad.shape[1]
        * pre_grad.shape[2]
        * pre_grad.shape[3]
        * lax.axis_size("tm")
        * lax.axis_size("dp")
    )
    scale = 1.0 / math.sqrt(total)
    return (features, clips_grad, kernel_sum * scale, bias_sum * scale)


def solution(mesh):
    in_specs = (P("dp", "tm", None, None, None), P(), P(), P("dp", "tm", None, None, None))
    out_specs = (P("dp", "tm", None, None, None), P("dp", "tm", None, None, None), P(), P())
    return jax.shard_map(local, mesh=mesh, in_specs=in_specs, out_specs=out_specs, check_vma=False)
```

profile of v0, /device:TPU:0, one launch (start us, length us, event | category | flops | bytes accessed | tf_op | source)
XLA Modules:
  0.0 229.5 jit_solution(3217730756475880015)
XLA Ops:
  7.2 0.0 copy-start
  7.2 0.0 all-reduce.3.cloned.1.call-start
  7.2 1.4 slice.6
  8.6 4.9 %collective-permute-start = (bf16[1,2,32,64,128]{4,3,2,1,0:T(8,128)(2,1)S(1)}, bf16[1,2,32,64,128]{4,3,2,1,0:T(8,128)(2,1)S(1)}, u32[]{:S(2)}, u32[]{:S(2)}) collective-permute-start(bf16[1,2,32,64,128]{4,3,2,1,0:T(8,128)(2,1)S(1)} %slice.6), channel_id=1, source_target_pairs={{0,8},{8,16},{16,24},{1,9},{9,17},{17,25},{2,10},{10,18},{18,26},{... | collective-permute-start | bytes 3145736 | tf_op jit(solution)/shard_map/ppermute | solution.py:12
  13.6 22.3 %collective-permute-done = bf16[1,2,32,64,128]{4,3,2,1,0:T(8,128)(2,1)S(1)} collective-permute-done((bf16[1,2,32,64,128]{4,3,2,1,0:T(8,128)(2,1)S(1)}, bf16[1,2,32,64,128]{4,3,2,1,0:T(8,128)(2,1)S(1)}, u32[]{:S(2)}, u32[]{:S(2)}) %collective-permute-start) | collective-permute-done | bytes 1048608 | tf_op jit(solution)/shard_map/ppermute | solution.py:12
  35.9 2.2 copy_dynamic-update-slice_fusion.1
  38.1 6.7 %copy_dynamic-update-slice_fusion = bf16[1,6,32,64,128]{4,0,3,2,1:T(2,128)(2,1)S(1)} fusion(bf16[1,6,32,64,128]{4,0,3,2,1:T(2,128)(2,1)S(1)} %copy_dynamic-update-slice_fusion.1, bf16[1,4,32,64,128]{4,3,2,1,0:T(8,128)(2,1)} %param.4), kind=kLoop, calls=%fused_computation.9 | loop fusion | bytes 6291456 | tf_op jit(solution)/shard_map/concatenate | solution.py:55
  44.9 3.7 %copy.53 = bf16[1,6,32,64,128]{4,2,3,1,0:T(8,128)(2,1)S(1)} copy(bf16[1,6,32,64,128]{4,0,3,2,1:T(2,128)(2,1)S(1)} %copy_dynamic-update-slice_fusion) | data formatting | bytes 6291456
  48.5 0.8 pad.5.clone
  49.3 2.7 %copy.31 = bf16[6,32,1,8,10,128]{5,3,4,1,0,2:T(8,128)(2,1)S(1)} copy(bf16[6,32,1,8,10,128]{5,1,4,3,0,2:T(8,128)(2,1)S(1)} %bitcast.45) | data formatting | bytes 7864320 | tf_op jit(solution)/shard_map/conv_general_dilated | solution.py:16
  52.0 0.2 slice.14
  52.3 3.8 %add_multiply_fusion = (f32[2,16,8,5,256]{4,2,3,1,0:T(8,128)S(1)}, bf16[2,16,8,5,256]{4,2,3,1,0:T(8,128)(2,1)}) fusion(f32[256]{0:T(256)S(1)} %copy-done.6, bf16[3,3,3,128,256]{4,3,2,1,0:T(8,128)(2,1)S(1)} %copy-done, bf16[6,32,1,7,2,128]{5,3,4,1,0,2:T(8,128)(2,1)S(1)} %slice.14, bf16[6,32,1,8,10,128]{5,3,4,1,0,2:T(8,128)(2,1)S(1)} %copy.31, ...), kind=kOutput, calls=%fused_computation.18 | convolution fusion | flops 2235498496 | bytes 8356904 | tf_op jit(solution)/shard_map/conv_general_dilated | solution.py:16
  56.1 0.4 copy.34
  56.5 0.6 copy-done.3
  57.1 1.0 convert_reduce_fusion
  58.1 17.5 %fusion.14 = f32[3,3,3,128,256]{4,3,2,1,0:T(8,128)} fusion(bf16[1,6,32,64,128]{4,0,3,2,1:T(2,128)(2,1)} %copy-done.1, bf16[1,2,16,32,256]{4,2,3,1,0:T(8,128)(2,1)S(1)} %get-tuple-element.13), kind=kOutput, calls=%fused_computation.26 | convolution fusion | flops 1755709440 | bytes 7208960 | tf_op jit(solution)/shard_map/conv_general_dilated | solution.py:40
  75.6 0.0 all-reduce.3.cloned.1.call-update
  75.7 1.4 collective-permute-start.1
  77.1 0.1 copy.32
  77.4 0.2 copy.36
  77.6 0.1 fusion.48
  77.7 1.0 copy.41
  78.6 46.1 %psum.15 = f32[256]{0:T(256)S(1)} all-reduce(f32[256]{0:T(256)S(1)} %copy-done.5), channel_id=1, replica_groups=mesh['tm'=4,'dp'=8] {'tm','dp'}, use_global_device_ids=true, to_apply=%region_2.3 | all-reduce | flops 256 | bytes 2048 | tf_op jit(solution)/shard_map/psum | solution.py:69
  124.7 0.6 broadcast_multiply_fusion.1
  125.3 0.1 copy.38
  125.5 2.5 %convolution_select_fusion = f32[2,32,8,10,128]{4,2,3,1,0:T(8,128)S(1)} fusion(bf16[3,3,3,128,256]{4,3,2,1,0:T(8,128)(2,1)S(1)} %copy-done, pred[8,10]{0,1:T(8,128)(4,1)S(1)} %copy-done.4, bf16[1,16,1,7,1,256]{5,3,4,1,2,0:T(8,128)(2,1)S(1)} %slice.19, bf16[1,16,1,8,5,256]{5,3,4,1,2,0:T(8,128)(2,1)S(1)} %copy.38), kind=kOutput, calls=%fused_computation.15 | convolution fusion | flops 741081088 | bytes 4776016 | tf_op jit(solution)/shard_map/conv_general_dilated | solution.py:28
  127.9 5.0 %add_convert_fusion = bf16[4,32,8,10,128]{4,2,3,1,0:T(8,128)(2,1)S(1)} fusion(f32[2,32,8,10,128]{4,2,3,1,0:T(8,128)S(1)} %convolution_select_fusion, pred[8,10]{0,1:T(8,128)(4,1)S(1)} %copy-done.4, bf16[3,3,3,128,256]{4,3,2,1,0:T(8,128)(2,1)S(1)} %copy-done, bf16[2,16,8,6,256]{4,2,3,1,0:T(8,128)(2,1)S(1)} %fusion.48), kind=kOutput, calls=%fused_computation.2 | convolution fusion | flops 1482424320 | bytes 7798864 | tf_op jit(solution)/shard_map/conv_general_dilated | solution.py:28
  132.9 0.7 copy.39
  133.6 0.4 slice_bitcast_fusion
  134.0 2.1 copy.42
  136.1 82.3 %all-reduce.3.cloned.1.call-done = f32[3,3,3,128,256]{4,3,2,1,0:T(8,128)} async-done(((f32[3,3,3,128,256]{4,3,2,1,0:T(8,128)}), f32[3,3,3,128,256]{4,3,2,1,0:T(8,128)}) %all-reduce.3.cloned.1.call-update) | async-done | bytes 3538960 | tf_op jit(solution)/shard_map/psum | solution.py:69
  218.4 4.3 %broadcast_multiply_fusion = f32[3,3,3,128,256]{4,3,2,1,0:T(8,128)} fusion(f32[3,3,3,128,256]{4,3,2,1,0:T(8,128)} %all-reduce.3.cloned.1.call-done), kind=kLoop, calls=%fused_computation.14 | loop fusion | flops 884736 | bytes 7077888 | tf_op jit(solution)/shard_map/mul | solution.py:79
  (21 shorter events, 0.2 us)
Async XLA Ops:
  7.2 45.1 %copy-start = (bf16[3,3,3,128,256]{4,3,2,1,0:T(8,128)(2,1)S(1)}, bf16[3,3,3,128,256]{4,3,2,1,0:T(8,128)(2,1)}, u32[]{:S(2)}) copy-start(bf16[3,3,3,128,256]{4,3,2,1,0:T(8,128)(2,1)} %param.5) | copy-start | bytes 5308420
  7.2 211.2 %all-reduce.3.cloned.1.call-start = ((), (), s32[]{:S(2)}) async-start(), calls=%async_computation | async-start | bytes 7077888 | tf_op jit(solution)/shard_map/psum | solution.py:69
  8.6 27.2 %collective-permute-start = (bf16[1,2,32,64,128]{4,3,2,1,0:T(8,128)(2,1)S(1)}, bf16[1,2,32,64,128]{4,3,2,1,0:T(8,128)(2,1)S(1)}, u32[]{:S(2)}, u32[]{:S(2)}) collective-permute-start(bf16[1,2,32,64,128]{4,3,2,1,0:T(8,128)(2,1)S(1)} %slice.6), channel_id=1, source_target_pairs={{0,8},{8,16},{16,24},{1,9},{9,17},{17,25},{2,10},{10,18},{18,26},{... | collective-permute-start | bytes 3145736 | tf_op jit(solution)/shard_map/ppermute | solution.py:12
  44.8 3.7 %copy-start.1 = (bf16[1,6,32,64,128]{4,0,3,2,1:T(2,128)(2,1)}, bf16[1,6,32,64,128]{4,0,3,2,1:T(2,128)(2,1)S(1)}, u32[]{:S(2)}) copy-start(bf16[1,6,32,64,128]{4,0,3,2,1:T(2,128)(2,1)S(1)} %copy_dynamic-update-slice_fusion) | copy-start | bytes 9437188
  49.3 3.0 %copy-start.6 = (f32[256]{0:T(256)S(1)}, f32[256]{0:T(256)}, u32[]{:S(2)}) copy-start(f32[256]{0:T(256)} %param.6) | copy-start | bytes 3076
  49.3 3.0 %copy-start.7 = (pred[8,5]{0,1:T(8,128)(4,1)S(1)}, pred[8,5]{0,1:T(8,128)(4,1)}, u32[]{:S(2)}) copy-start(pred[8,5]{0,1:T(8,128)(4,1)} %constant.25) | copy-start | bytes 124
  56.1 1.0 copy-start.3
  75.6 1.5 copy-start.2
  75.7 49.6 %collective-permute-start.1 = (bf16[1,1,16,32,256]{4,2,3,1,0:T(8,128)(2,1)S(1)}, bf16[1,1,16,32,256]{4,2,3,1,0:T(8,128)(2,1)S(1)}, u32[]{:S(2)}, u32[]{:S(2)}) collective-permute-start(bf16[1,1,16,32,256]{4,2,3,1,0:T(8,128)(2,1)S(1)} %slice.18), channel_id=1, source_target_pairs={{8,0},{16,8},{24,16},{9,1},{17,9},{25,17},{10,2},{18,10},{26,18},{... | collective-permute-start | bytes 786440 | tf_op jit(solution)/shard_map/ppermute | solution.py:12
  77.3 1.4 copy-start.5
  77.4 48.1 %copy-start.4 = (pred[8,10]{0,1:T(8,128)(4,1)S(1)}, pred[8,10]{0,1:T(8,128)(4,1)}, u32[]{:S(2)}) copy-start(pred[8,10]{0,1:T(8,128)(4,1)} %constant.26) | copy-start | bytes 244
Sparse Core Ops, SparseCore 0:
  75.8 142.5 all-reduce.2
where the time goes:
time: 230 us
  waiting for transfers between devices  105 us (46%)
  blocking collectives  46.1 us (20%)
  matrix products  28.8 us (13%)
  local copies, waits for them, and re-layouts  23.5 us (10%)
  between operations  14.3 us (6%)
  starting transfers between devices  6.37 us (3%)
  other arithmetic  5.85 us (3%)
    psum x1, waiting for transfers between devices, local(): kernel_sum, bias_sum = lax.psum((kernel_part, bias_part), ('tm', 'dp'))  82.3 us
    psum x1, blocking collectives, local(): kernel_sum, bias_sum = lax.psum((kernel_part, bias_part), ('tm', 'dp'))  46.1 us
    ppermute x2, waiting for transfers between devices, passed_along(): lax.ppermute(value, axis, [(source, source + steps) for source in range(f...  22.3 us
    conv_general_dilated x1, matrix products, kernel_conv(): lax.conv_general_dilated(extended, pre_grad, (1, 1, 1), ((0, -1), (1, 0),...  17.5 us
    unnamed x20, local copies, waits for them, and re-layouts  9.64 us
    concatenate x2, local copies, waits for them, and re-layouts, local(): extended = jnp.concatenate([prior, clips], axis=1)  7.48 us
    conv_general_dilated x2, matrix products, back_conv(): lax.conv_general_dilated(grads, flipped, (1, 1, 1), ((low, high), (1, 2),...  7.42 us
    ppermute x2, starting transfers between devices, passed_along(): lax.ppermute(value, axis, [(source, source + steps) for source in range(f...  6.33 us
  transfers between devices with their start and end apart: 3, of which 2 were waited for; matrix products, arithmetic and copies ran while one was open for 6% of the time, Pallas kernels for 0%

commit v1 on v0

v1 whole, which is shorter than its diff:
```python
import functools
import math

import jax
import jax.numpy as jnp
from jax import lax
from jax.experimental import pallas as pl
from jax.experimental.pallas import tpu as pltpu
from jax.sharding import PartitionSpec as P

MESH = pl.DeviceIdType.MESH
BF = jnp.bfloat16
F32 = jnp.float32


def passed_along(value, axis, steps):
    count = lax.axis_size(axis)
    first, last = (max(0, -steps), min(count, count - steps))
    return lax.ppermute(value, axis, [(source, source + steps) for source in range(first, last)])


def sum_kernel(tms, zs, part, out, wire, got1, own1, send2, got2, own2, send3, got3, sems_s, sems_r):
    tm = lax.axis_index("tm")
    dp = lax.axis_index("dp")
    core = dp % 2
    z = dp // 2
    mate = dp + 1 - 2 * core
    half = part.shape[0] // 2
    quarter = half // tms
    piece = quarter // zs

    mates = [{"tm": tm, "dp": mate}]
    plane = [{"tm": (tm + d) % tms, "dp": dp} for d in range(1, tms)]
    line = [{"tm": tm, "dp": ((z + d) % zs) * 2 + core} for d in range(1, zs)]
    everyone = mates + plane + line

    barrier = pltpu.get_barrier_semaphore()
    for other in everyone:
        pl.semaphore_signal(barrier, inc=1, device_id=other, device_id_type=MESH)

    def rows(start, count):
        return pl.ds(pl.multiple_of(start, 16), count)

    wire[...] = part[rows((1 - core) * half, half), :].astype(BF)
    pl.semaphore_wait(barrier, len(everyone))

    def copy(src, dst, slot, to):
        made = pltpu.make_async_remote_copy(
            src_ref=src,
            dst_ref=dst,
            send_sem=sems_s.at[slot],
            recv_sem=sems_r.at[slot],
            device_id=to,
            device_id_type=MESH,
        )
        made.start()
        return made

    slot = 0
    first = copy(wire, got1, slot, mates[0])
    slot += 1
    first.wait()
    own1[...] = part[rows(core * half, half), :] + got1[...].astype(F32)
    send2[...] = own1[...].astype(BF)

    copies = []
    for d in range(1, tms):
        src = send2.at[rows(((tm + d) % tms) * quarter, quarter), :]
        copies.append(copy(src, got2.at[d - 1], slot, plane[d - 1]))
        slot += 1
    for made in copies:
        made.wait()
    total = own1[rows(tm * quarter, quarter), :]
    for d in range(1, tms):
        total = total + got2[d - 1].astype(F32)
    own2[...] = total
    send3[...] = total.astype(BF)

    copies = []
    for d in range(1, zs):
        src = send3.at[rows(((z + d) % zs) * piece, piece), :]
        copies.append(copy(src, got3.at[d - 1], slot, line[d - 1]))
        slot += 1
    for made in copies:
        made.wait()
    total = own2[rows(z * piece, piece), :]
    for d in range(1, zs):
        total = total + got3[d - 1].astype(F32)
    at3 = core * half + tm * quarter + z * piece
    out[rows(at3, piece), :] = total.astype(BF)

    for start, count, group in (
        (at3, piece, line),
        (core * half + tm * quarter, quarter, plane),
        (core * half, half, mates),
    ):
        copies = []
        for other in group:
            block = out.at[rows(start, count), :]
            copies.append(copy(block, block, slot, other))
            slot += 1
        for made in copies:
            made.wait()


def summed(part):
    tms = lax.axis_size("tm")
    zs = lax.axis_size("dp") // 2
    rows, cols = part.shape
    half = rows // 2
    quarter = half // tms
    piece = quarter // zs
    count = 2 * (1 + (tms - 1) + (zs - 1))
    return pl.pallas_call(
        functools.partial(sum_kernel, tms, zs),
        out_shape=jax.ShapeDtypeStruct((rows, cols), BF),
        in_specs=[pl.BlockSpec(memory_space=pltpu.VMEM)],
        out_specs=pl.BlockSpec(memory_space=pltpu.VMEM),
        scratch_shapes=[
            pltpu.VMEM((half, cols), BF),
            pltpu.VMEM((half, cols), BF),
            pltpu.VMEM((half, cols), F32),
            pltpu.VMEM((half, cols), BF),
            pltpu.VMEM((max(1, tms - 1), quarter, cols), BF),
            pltpu.VMEM((quarter, cols), F32),
            pltpu.VMEM((quarter, cols), BF),
            pltpu.VMEM((max(1, zs - 1), piece, cols), BF),
            pltpu.SemaphoreType.DMA((count,)),
            pltpu.SemaphoreType.DMA((count,)),
        ],
        compiler_params=pltpu.CompilerParams(
            collective_id=0, has_side_effects=True, vmem_limit_bytes=32 * 1024 * 1024
        ),
    )(part)


def forward_conv(frames, weight):
    return lax.conv_general_dilated(
        frames,
        weight,
        (2, 2, 2),
        ((0, 0), (1, 1), (1, 1)),
        dimension_numbers=("NDHWC", "DHWIO", "NDHWC"),
        preferred_element_type=F32,
    )


def back_conv(grads, weight, low, high):
    flipped = weight[::-1, ::-1, ::-1]
    return lax.conv_general_dilated(
        grads,
        flipped,
        (1, 1, 1),
        ((low, high), (1, 2), (1, 2)),
        lhs_dilation=(2, 2, 2),
        dimension_numbers=("NDHWC", "DHWOI", "NDHWC"),
        preferred_element_type=F32,
    )


def kernel_conv(clips, grads):
    return lax.conv_general_dilated(
        clips,
        grads,
        (1, 1, 1),
        ((2, 1), (1, 0), (1, 0)),
        rhs_dilation=(2, 2, 2),
        dimension_numbers=("CDHWN", "IDHWO", "DHWNC"),
        preferred_element_type=F32,
    )


def local(clips, weight, bias, out_grad):
    frames = clips.shape[1]
    spill = forward_conv(clips[:, frames - 2 :], weight[:2]).astype(BF)
    prior = passed_along(spill, "tm", 1)
    later_pre = forward_conv(clips[:, : frames - 1], weight)
    first_pre = forward_conv(clips[:, :1], weight[2:]) + prior.astype(F32)
    pre = jnp.concatenate([first_pre, later_pre], axis=1) + bias
    sig = jax.nn.sigmoid(pre)
    features = (pre * sig).astype(BF)
    pre_grad = (out_grad.astype(F32) * (sig * (1.0 + pre * (1.0 - sig)))).astype(BF)
    following = passed_along(pre_grad[:, :1], "tm", -1)
    grads = jnp.concatenate([pre_grad, following], axis=1)
    kernel_part = kernel_conv(clips, grads)
    bias_part = jnp.sum(pre_grad.astype(F32), axis=(0, 1, 2, 3))

    c_out = bias.shape[0]
    taps = kernel_part.size // c_out
    devices = lax.axis_size("tm") * lax.axis_size("dp")
    step = 16 * devices
    rows = -(-(taps + 2) // step) * step
    high = bias_part.astype(BF).astype(F32)
    tail = jnp.concatenate(
        [high[None], (bias_part - high)[None], jnp.zeros((rows - taps - 2, c_out), F32)]
    )
    total = summed(jnp.concatenate([kernel_part.reshape(taps, c_out), tail]))
    clips_grad = back_conv(grads, weight, 0, 1).astype(BF)

    positions = pre_grad.size // c_out * devices
    scale = 1.0 / math.sqrt(positions)
    kernel_grad = total[:taps].astype(F32).reshape(kernel_part.shape) * scale
    bias_sum = total[taps].astype(F32) + total[taps + 1].astype(F32)
    return (features, clips_grad, kernel_grad, bias_sum * scale)


def solution(mesh):
    in_specs = (P("dp", "tm", None, None, None), P(), P(), P("dp", "tm", None, None, None))
    out_specs = (P("dp", "tm", None, None, None), P("dp", "tm", None, None, None), P(), P())
    return jax.shard_map(local, mesh=mesh, in_specs=in_specs, out_specs=out_specs, check_vma=False)
```

time: 230 us -> 133 us (0.58)
  waiting for transfers between devices: 105 us -> 8.35 us
  blocking collectives: 46.1 us -> 0 us
  Pallas kernels: 0 us -> 42.2 us
  matrix products: 28.8 us -> 54.1 us
  between operations: 14.3 us -> 0.86 us
  local copies, waits for them, and re-layouts: 23.5 us -> 15.5 us
    psum x1 -> x0, waiting for transfers between devices: 82.3 us -> none  [local(): kernel_sum, bias_sum = lax.psum((kernel_part, bias_part), ('tm', 'dp'))]
    psum x1 -> x0, blocking collectives: 46.1 us -> none  [local(): kernel_sum, bias_sum = lax.psum((kernel_part, bias_part), ('tm', 'dp'))]
    pallas_call x0 -> x1, Pallas kernels: none -> 42.2 us  [summed(): pl.pallas_call(functools.partial(sum_kernel, tms, zs), out_shape=jax.Shap...]
    conv_general_dilated x2 -> x4, matrix products: 21.3 us -> 49.1 us  [the longest x1 30.5 us: kernel_conv(): lax.conv_general_dilated(clips, grads, (1, 1, 1), ((2, 1), (1, 0), (1, 0)...]
    ppermute x2, waiting for transfers between devices: 22.3 us -> 8.35 us  [passed_along(): lax.ppermute(value, axis, [(source, source + steps) for source in range(f...]
    unnamed x20 -> x18, local copies, waits for them, and re-layouts: 9.64 us -> 5.59 us
    conv_general_dilated x2, local copies, waits for them, and re-layouts: 2.93 us -> 0.09 us  [forward_conv(): lax.conv_general_dilated(frames, weight, (2, 2, 2), ((0, 0), (1, 1), (1,...]
    conv_general_dilated x2 -> x1, matrix products: 7.42 us -> 4.98 us  [back_conv(): lax.conv_general_dilated(grads, flipped, (1, 1, 1), ((low, high), (1, 2),...]
  transfers between devices with their start and end apart: 3 -> 2, of which waited for: 2 -> 1; matrix products, arithmetic and copies ran while one was open for 6% -> 9% of each run, Pallas kernels for 0% -> 0%
where the time goes in v1:
time: 133 us; the launch traced here: 132 us
  matrix products  54.1 us (41%)
  Pallas kernels  42.2 us (32%)
  local copies, waits for them, and re-layouts  15.5 us (12%)
  waiting for transfers between devices  8.35 us (6%)
  starting transfers between devices  6.33 us (5%)
  other arithmetic  5.15 us (4%)
    pallas_call x1, Pallas kernels, summed(): pl.pallas_call(functools.partial(sum_kernel, tms, zs), out_shape=jax.Shap...  42.2 us
    conv_general_dilated x1, matrix products, kernel_conv(): lax.conv_general_dilated(clips, grads, (1, 1, 1), ((2, 1), (1, 0), (1, 0)...  30.5 us
    conv_general_dilated x3, matrix products, forward_conv(): lax.conv_general_dilated(frames, weight, (2, 2, 2), ((0, 0), (1, 1), (1,...  18.6 us
    ppermute x2, waiting for transfers between devices, passed_along(): lax.ppermute(value, axis, [(source, source + steps) for source in range(f...  8.35 us
    concatenate x1, local copies, waits for them, and re-layouts, local(): total = summed(jnp.concatenate([kernel_part.reshape(taps, c_out), tail]))  7.6 us
    ppermute x2, starting transfers between devices, passed_along(): lax.ppermute(value, axis, [(source, source + steps) for source in range(f...  6.33 us
    unnamed x18, local copies, waits for them, and re-layouts  5.59 us
    conv_general_dilated x1, matrix products, back_conv(): lax.conv_general_dilated(grads, flipped, (1, 1, 1), ((low, high), (1, 2),...  4.98 us
  transfers between devices with their start and end apart: 2, of which 1 were waited for; matrix products, arithmetic and copies ran while one was open for 9% of the time, Pallas kernels for 0%

profile of v1, /device:TPU:0, one launch (start us, length us, event | category | flops | bytes accessed | tf_op | source)
XLA Modules:
  0.0 132.4 jit_solution(1278843887054641706)
XLA Ops:
  0.6 0.0 copy-start.5
  0.7 6.5 %fusion.6 = bf16[1,1,16,32,256]{4,0,3,2,1:T(2,128)(2,1)S(1)} fusion(bf16[1,4,32,64,128]{4,3,2,1,0:T(8,128)(2,1)} %param.4, bf16[3,3,3,128,256]{4,3,2,1,0:T(8,128)(2,1)} %param.5), kind=kOutput, calls=%fused_computation.10 | convolution fusion | flops 585236480 | bytes 3538944 | tf_op jit(solution)/shard_map/conv_general_dilated | solution.py:138
  7.2 4.9 %collective-permute-start = (bf16[1,1,16,32,256]{4,3,2,1,0:T(8,128)(2,1)S(1)}, bf16[1,1,16,32,256]{4,3,2,1,0:T(8,128)(2,1)S(1)}, u32[]{:S(2)}, u32[]{:S(2)}) collective-permute-start(bf16[1,1,16,32,256]{4,3,2,1,0:T(8,128)(2,1)S(1)} %copy.53), channel_id=1, source_target_pairs={{0,8},{8,16},{16,24},{1,9},{9,17},{17,25},{2,10},{10,18},{18,26},{... | collective-permute-start | bytes 786440 | tf_op jit(solution)/shard_map/ppermute | solution.py:19
  12.1 9.6 %fusion.4 = f32[1,1,16,32,256]{4,0,3,2,1:T(1,128)S(1)} fusion(bf16[3,3,3,128,256]{4,3,2,1,0:T(8,128)(2,1)S(1)} %copy-done.5, bf16[1,4,32,64,128]{4,3,2,1,0:T(8,128)(2,1)S(1)} %copy-done.4), kind=kOutput, calls=%fused_computation.8 | convolution fusion | flops 877854720 | bytes 4390912 | tf_op jit(solution)/shard_map/conv_general_dilated | solution.py:138
  21.8 0.0 copy-start.2
  21.8 0.0 copy-start.3
  21.8 2.5 %fusion.8 = f32[1,1,16,32,256]{4,0,3,2,1:T(1,128)S(1)} fusion(bf16[1,4,32,64,128]{4,3,2,1,0:T(8,128)(2,1)S(1)} %copy-done.4, bf16[3,3,3,128,256]{4,3,2,1,0:T(8,128)(2,1)S(1)} %copy-done.5), kind=kOutput, calls=%fused_computation.12 | convolution fusion | flops 292618240 | bytes 3211264 | tf_op jit(solution)/shard_map/conv_general_dilated | solution.py:138
  24.3 0.0 collective-permute-done
  24.3 0.1 copy_add_fusion
  24.4 0.0 copy-done.2
  24.4 1.3 convert_reduce_fusion
  25.7 1.5 %collective-permute-start.1 = (bf16[1,1,16,32,256]{4,3,2,1,0:T(8,128)(2,1)S(1)}, bf16[1,1,16,32,256]{4,3,2,1,0:T(8,128)(2,1)S(1)}, u32[]{:S(2)}, u32[]{:S(2)}) collective-permute-start(bf16[1,1,16,32,256]{4,3,2,1,0:T(8,128)(2,1)S(1)} %slice.29), channel_id=1, source_target_pairs={{8,0},{16,8},{24,16},{9,1},{17,9},{25,17},{10,2},{18,10},{26,18},{... | collective-permute-start | bytes 786440 | tf_op jit(solution)/shard_map/ppermute | solution.py:19
  27.2 8.3 %collective-permute-done.1 = bf16[1,1,16,32,256]{4,3,2,1,0:T(8,128)(2,1)S(1)} collective-permute-done((bf16[1,1,16,32,256]{4,3,2,1,0:T(8,128)(2,1)S(1)}, bf16[1,1,16,32,256]{4,3,2,1,0:T(8,128)(2,1)S(1)}, u32[]{:S(2)}, u32[]{:S(2)}) %collective-permute-start.1) | collective-permute-done | bytes 262176 | tf_op jit(solution)/shard_map/ppermute | solution.py:19
  35.6 1.0 pad_maximum_fusion
  36.5 30.5 %fusion.1 = f32[3,3,3,128,256]{4,3,2,1,0:T(8,128)S(1)} fusion(bf16[1,3,16,32,256]{4,3,2,1,0:T(8,128)(2,1)S(1)} %get-tuple-element.19, bf16[1,4,32,64,128]{4,3,2,1,0:T(8,128)(2,1)S(1)} %copy-done.4), kind=kOutput, calls=%fused_computation.5 | convolution fusion | flops 1755709440 | bytes 6422528 | tf_op jit(solution)/shard_map/conv_general_dilated | solution.py:162
  67.1 0.7 broadcast_in_dim.2
  67.7 7.6 %concatenate.23.part = f32[3584,256]{1,0:T(8,128)} concatenate(f32[3456,256]{1,0:T(8,128)S(1)} %bitcast.23, f32[1,256]{1,0:T(1,128)S(1)} %get-tuple-element.22, f32[1,256]{1,0:T(1,128)S(1)} %get-tuple-element.21, f32[126,256]{1,0:T(8,128)} %broadcast_in_dim.2), dimensions={0} | concatenate | bytes 7340032 | tf_op jit(solution)/shard_map/concatenate | solution.py:197
  75.3 2.0 %copy-done = f32[3584,256]{1,0:T(8,128)S(1)} copy-done((f32[3584,256]{1,0:T(8,128)S(1)}, f32[3584,256]{1,0:T(8,128)}, u32[]{:S(2)}) %copy-start) | copy-done | bytes 3670040
  77.4 42.2 %shard_map.75 = bf16[3584,256]{1,0:T(8,128)(2,1)S(1)} custom-call(f32[3584,256]{1,0:T(8,128)S(1)} %copy-done), custom_call_target="tpu_custom_call" | custom-call | tf_op jit(solution)/shard_map/pallas_call | solution.py:114
  119.6 0.6 add_multiply_fusion
  120.1 2.1 %convert_multiply_fusion = f32[3456,256]{1,0:T(8,128)} fusion(bf16[3584,256]{1,0:T(8,128)(2,1)S(1)} %shard_map.75), kind=kLoop, calls=%fused_computation.1 | loop fusion | flops 1769472 | bytes 5308416 | tf_op jit(solution)/shard_map/mul | solution.py:202
  122.2 0.4 copy.40
  122.7 0.1 pad.clone
  122.8 0.0 copy-start.6
  122.8 0.0 copy-start.7
  122.8 0.3 copy.35
  123.2 0.1 fusion.29
  123.3 0.9 copy-done.6
  124.2 5.0 %select_convert_fusion = bf16[4,32,8,10,128]{4,2,3,1,0:T(8,128)(2,1)S(1)} fusion(pred[8,10]{0,1:T(8,128)(4,1)S(1)} %copy-done.7, bf16[3,3,3,128,256]{4,3,2,1,0:T(8,128)(2,1)S(1)} %copy-done.6, bf16[3,16,8,6,256]{4,2,3,1,0:T(8,128)(2,1)S(1)} %fusion.29), kind=kOutput, calls=%fused_computation | convolution fusion | flops 2220359680 | bytes 5570640 | tf_op jit(solution)/shard_map/conv_general_dilated | solution.py:150
  129.2 0.7 copy.36
  129.9 0.4 slice_bitcast_fusion
  130.3 2.1 %copy.39 = bf16[1,4,32,64,128]{4,3,2,1,0:T(8,128)(2,1)} copy(bf16[1,4,32,64,128]{4,2,3,1,0:T(8,128)(2,1)S(1)} %slice_bitcast_fusion) | data formatting | bytes 4194304
  (13 shorter events, 0.2 us)
Async XLA Ops:
  0.6 11.4 %copy-start.5 = (bf16[3,3,3,128,256]{4,3,2,1,0:T(8,128)(2,1)S(1)}, bf16[3,3,3,128,256]{4,3,2,1,0:T(8,128)(2,1)}, u32[]{:S(2)}) copy-start(bf16[3,3,3,128,256]{4,3,2,1,0:T(8,128)(2,1)} %param.5) | copy-start | bytes 5308420
  0.6 11.4 %copy-start.4 = (bf16[1,4,32,64,128]{4,3,2,1,0:T(8,128)(2,1)S(1)}, bf16[1,4,32,64,128]{4,3,2,1,0:T(8,128)(2,1)}, u32[]{:S(2)}) copy-start(bf16[1,4,32,64,128]{4,3,2,1,0:T(8,128)(2,1)} %param.4) | copy-start | bytes 6291460
  7.2 17.1 %collective-permute-start = (bf16[1,1,16,32,256]{4,3,2,1,0:T(8,128)(2,1)S(1)}, bf16[1,1,16,32,256]{4,3,2,1,0:T(8,128)(2,1)S(1)}, u32[]{:S(2)}, u32[]{:S(2)}) collective-permute-start(bf16[1,1,16,32,256]{4,3,2,1,0:T(8,128)(2,1)S(1)} %copy.53), channel_id=1, source_target_pairs={{0,8},{8,16},{16,24},{1,9},{9,17},{17,25},{2,10},{10,18},{18,26},{... | collective-permute-start | bytes 786440 | tf_op jit(solution)/shard_map/ppermute | solution.py:19
  21.8 2.6 %copy-start.2 = (bf16[1,2,16,32,256]{4,3,2,1,0:T(8,128)(2,1)S(1)}, bf16[1,2,16,32,256]{4,3,2,1,0:T(8,128)(2,1)}, u32[]{:S(2)}) copy-start(bf16[1,2,16,32,256]{4,3,2,1,0:T(8,128)(2,1)} %param.7) | copy-start | bytes 1572868
  21.8 2.6 %copy-start.3 = (f32[256]{0:T(256)S(1)}, f32[256]{0:T(256)}, u32[]{:S(2)}) copy-start(f32[256]{0:T(256)} %param.6) | copy-start | bytes 3076
  25.7 9.8 %collective-permute-start.1 = (bf16[1,1,16,32,256]{4,3,2,1,0:T(8,128)(2,1)S(1)}, bf16[1,1,16,32,256]{4,3,2,1,0:T(8,128)(2,1)S(1)}, u32[]{:S(2)}, u32[]{:S(2)}) collective-permute-start(bf16[1,1,16,32,256]{4,3,2,1,0:T(8,128)(2,1)S(1)} %slice.29), channel_id=1, source_target_pairs={{8,0},{16,8},{24,16},{9,1},{17,9},{25,17},{10,2},{18,10},{26,18},{... | collective-permute-start | bytes 786440 | tf_op jit(solution)/shard_map/ppermute | solution.py:19
  75.3 2.0 %copy-start = (f32[3584,256]{1,0:T(8,128)S(1)}, f32[3584,256]{1,0:T(8,128)}, u32[]{:S(2)}) copy-start(f32[3584,256]{1,0:T(8,128)} %concatenate.23.part) | copy-start | bytes 11010052
  120.1 2.1 %copy-start.1 = (bf16[3,16,1,32,256]{4,3,1,0,2:T(8,128)(2,1)S(1)}, bf16[3,16,1,32,256]{4,3,1,0,2:T(8,128)(2,1)}, u32[]{:S(2)}) copy-start(bf16[3,16,1,32,256]{4,3,1,0,2:T(8,128)(2,1)} %get-tuple-element.20) | copy-start | bytes 2359300
  122.8 1.5 %copy-start.6 = (bf16[3,3,3,128,256]{4,3,2,1,0:T(8,128)(2,1)S(1)}, bf16[3,3,3,128,256]{4,3,2,1,0:T(8,128)(2,1)}, u32[]{:S(2)}) copy-start(bf16[3,3,3,128,256]{4,3,2,1,0:T(8,128)(2,1)} %param.5) | copy-start | bytes 5308420
  122.8 1.5 %copy-start.7 = (pred[8,10]{0,1:T(8,128)(4,1)S(1)}, pred[8,10]{0,1:T(8,128)(4,1)}, u32[]{:S(2)}) copy-start(pred[8,10]{0,1:T(8,128)(4,1)} %constant.14) | copy-start | bytes 244
